TPU v7x, 512 devices: a whole 4x4x16 slice. The times are simulated.
512 devices in a mesh: space: 32 (over z, y_hi), scen: 16 (over x, y_lo, core).
Axes of the slice: x: 4, y: 4 (y_hi: 2, y_lo: 2; y = y_hi * 2 + y_lo), z: 16, core: 2. Of those that a mesh axis runs over, the one named last changes fastest.
Arguments:
- start_fraction: bfloat16 [64, 24, 65536], P('scen', None, 'space'), may hold values from 0 to 1
- ore_value: bfloat16 [64, 24, 65536], P('scen', None, 'space'), may hold values from -6 to 6
- dual_price: float32 [64, 24, 65536], P('scen', None, 'space'), may hold values from -3 to 3
- patterns: bfloat16 [3, 512, 512], replicated, may hold values from -0.15625 to 0.15625
- cone_list: int32 [128, 3], P('space'), may hold values from 0 to 127, as said below
- node_list: int32 [2, 64], replicated, may hold values from 0 to 15, as said below
- probability: float32 [64], replicated, may hold values from 0.5 to 2
Outputs:
- fraction: float32 [64, 24, 65536], P('scen', None, 'space')
- dual_out: float32 [64, 24, 65536], P('scen', None, 'space')
Inputs may be any that keep to these rules, and one draw needn't show every extreme that they name: `cone_list`: row i holds i, then tile i - 1 and tile i + 1 in an order drawn per tile; where a neighbour lies outside the slab the tile itself stands in its place. `node_list`: row 0 holds second-section nodes below 4, row 1 third-section nodes; every node holds a scenario, and scenarios that share a third-section node share their second-section node.
All inputs are finite; a program needn't handle non-finite values.
Results may differ from a plain program's by a relative error of at most 0.00079.
Values may be sent and summed in bfloat16 or wider, within the bound.
A program may use at most 64 MiB of HBM per device.

v0:
```python
import jax
import jax.numpy as jnp
from jax import lax
from jax.sharding import PartitionSpec as P

TILE = 512
SECTIONS = 4
NODES1 = 4
NODES2 = 16
ITERS = 2
PG_STEPS = 2


def extended_2(array, sides, width):
    for axis, dim in sides:
        size, length = (lax.axis_size(axis), array.shape[dim])
        up = [(i, (i + 1) % size) for i in range(size - 1)]
        down = [(j, i) for i, j in up]
        last = lax.slice_in_dim(array, length - width, length, axis=dim)
        first = lax.slice_in_dim(array, 0, width, axis=dim)
        before = lax.ppermute(last, axis, up)
        after = lax.ppermute(first, axis, down)
        array = jnp.concatenate([before, array, after], axis=dim)
    return array


def node_weights(nodes, weights_in, count):
    return (nodes[:, None] == jnp.arange(count)[None, :]).astype(jnp.float32) * weights_in[:, None]


def tree_center(fraction, node_list, probability):
    quarter = fraction.shape[1] // SECTIONS
    scen_local = fraction.shape[0]
    leaf_part = fraction[:, (SECTIONS - 1) * quarter :]
    offset = lax.axis_index("scen") * scen_local
    local_prob = lax.dynamic_slice_in_dim(probability, offset, scen_local, 0)
    local_nodes = lax.dynamic_slice_in_dim(node_list, offset, scen_local, 1)
    weight_one = node_weights(local_nodes[0], local_prob, NODES1)
    weight_two = node_weights(local_nodes[1], local_prob, NODES2)
    root_term = jnp.tensordot(
        local_prob, fraction[:, :quarter], axes=1, precision=lax.Precision.HIGHEST
    )
    first_term = jnp.tensordot(
        weight_one,
        fraction[:, quarter : 2 * quarter],
        axes=((0,), (0,)),
        precision=lax.Precision.HIGHEST,
    )
    second_term = jnp.tensordot(
        weight_two,
        fraction[:, 2 * quarter : 3 * quarter],
        axes=((0,), (0,)),
        precision=lax.Precision.HIGHEST,
    )
    root_sum, first_sum, second_sum = lax.psum((root_term, first_term, second_term), "scen")
    full_one = node_weights(node_list[0], probability, NODES1)
    full_two = node_weights(node_list[1], probability, NODES2)
    root_mean = root_sum / jnp.sum(probability)
    first_mean = first_sum / jnp.sum(full_one, axis=0)[:, None, None]
    second_mean = second_sum / jnp.sum(full_two, axis=0)[:, None, None]
    root_part = jnp.broadcast_to(root_mean[None], (scen_local, quarter, fraction.shape[2]))
    first_part = jnp.take(first_mean, local_nodes[0], axis=0)
    second_part = jnp.take(second_mean, local_nodes[1], axis=0)
    return jnp.concatenate([root_part, first_part, second_part, leaf_part], axis=1)


def descend(fraction, ore_value, dual_now, center, local_cone, patterns):
    rounded = fraction.astype(jnp.bfloat16)
    full_shape = fraction.shape
    tile_view = rounded.reshape(full_shape[0], full_shape[1], full_shape[2] // TILE, TILE)
    extended = extended_2(tile_view, (("space", 2),), 1)
    accumulated = jnp.zeros((fraction.size // TILE, TILE), jnp.float32)
    for cone_slot in range(3):
        picked = jnp.take(extended, local_cone[:, cone_slot], axis=2).reshape(-1, TILE)
        accumulated = accumulated + jnp.dot(
            picked, patterns[cone_slot], preferred_element_type=jnp.float32
        )
    cone_mix = accumulated.reshape(full_shape)
    gradient = (
        -ore_value.astype(jnp.float32)
        + dual_now
        + 1.0 * (fraction - center)
        + 1.0 * (fraction - cone_mix)
    )
    return jnp.clip(fraction - 0.4 * gradient, 0.0, 1.0)


def body(start_fraction, ore_value, dual_price, patterns, cone_list, node_list, probability):
    first_tile = lax.axis_index("space") * cone_list.shape[0]
    local_cone = cone_list - first_tile + 1
    fraction = start_fraction.astype(jnp.float32)
    dual_now = dual_price
    center = tree_center(fraction, node_list, probability)
    for ph_round in range(ITERS):
        for inner_step in range(PG_STEPS):
            fraction = descend(fraction, ore_value, dual_now, center, local_cone, patterns)
        center = tree_center(fraction, node_list, probability)
        dual_now = dual_now + 1.0 * (fraction - center)
    return (fraction, dual_now)


def solution(mesh):
    in_specs = (
        P("scen", None, "space"),
        P("scen", None, "space"),
        P("scen", None, "space"),
        P(),
        P("space", None),
        P(),
        P(),
    )
    out_specs = (P("scen", None, "space"), P("scen", None, "space"))
    return jax.shard_map(body, mesh=mesh, in_specs=in_specs, out_specs=out_specs, check_vma=False)
```

profile of v0, /device:TPU:1, one launch (start us, length us, event | category | flops | bytes accessed | tf_op | source)
XLA Modules:
  0.0 645.6 jit_solution(9549400603886811257)
XLA Ops:
  8.3 5.7 collective-permute-start
  21.5 51.5 %psum.63 = f32[6,2048]{1,0:T(8,128)S(1)} all-reduce(f32[6,2048]{1,0:T(8,128)S(1)} %bitcast.124), channel_id=1, replica_groups=mesh['space'=32,'scen'=16] {'scen'}, use_global_device_ids=true, to_apply=%region_0.0 | all-reduce | flops 12288 | bytes 98304 | tf_op jit(solution)/shard_map/psum | solution.py:55
  84.0 74.5 %all-reduce.11.cloned.1.call-done = (f32[16,6,2048]{2,0,1:T(8,128)}, f32[4,6,2048]{2,0,1:T(4,128)}) async-done(((f32[16,6,2048]{2,0,1:T(8,128)}, f32[4,6,2048]{2,0,1:T(4,128)}), (f32[16,6,2048]{2,0,1:T(8,128)}, f32[4,6,2048]{2,0,1:T(4,128)})) %all-reduce.11.cloned.1.call-update) | async-done | bytes 983056 | tf_op jit(solution)/shard_map/psum | solution.py:55
  162.3 2.6 gather_fusion.1
  166.1 2.4 gather_fusion
  170.6 3.9 fusion.109
  176.1 3.6 collective-permute-start.2
  183.0 3.7 collective-permute-done.3
  189.1 2.4 gather_fusion.6
  191.5 2.5 gather_fusion.7
  203.9 2.4 reshape.99
  206.3 3.9 fusion.107
  210.1 1.8 fusion.54
  213.0 2.0 reshape.100
  215.0 2.2 fusion.112
  217.9 4.8 collective-permute-start.4
  224.1 55.0 %psum.66 = f32[6,2048]{1,0:T(8,128)} all-reduce(f32[6,2048]{1,0:T(8,128)} %bitcast.125), channel_id=1, replica_groups=mesh['space'=32,'scen'=16] {'scen'}, use_global_device_ids=true, to_apply=%region_6.10 | all-reduce | flops 12288 | bytes 98304 | tf_op jit(solution)/shard_map/psum | solution.py:55
  279.2 2.1 broadcast_divide_fusion.7
  288.4 2.0 constant_dynamic-update-slice_fusion.7
  290.4 2.1 collective-permute-done.5
  294.0 2.5 gather_fusion.10
  296.5 2.4 gather_fusion.11
  298.9 2.5 gather_fusion.12
  303.6 1.8 reshape.101
  307.6 1.8 reshape.102
  311.6 1.8 reshape.103
  317.1 2.4 reshape.104
  319.4 104.0 %all-reduce.9.cloned.1.call-done = (f32[16,6,2048]{2,0,1:T(8,128)}, f32[4,6,2048]{2,0,1:T(4,128)}) async-done(((f32[16,6,2048]{2,0,1:T(8,128)}, f32[4,6,2048]{2,0,1:T(4,128)}), (f32[16,6,2048]{2,0,1:T(8,128)}, f32[4,6,2048]{2,0,1:T(4,128)})) %all-reduce.9.cloned.1.call-update) | async-done | bytes 983056 | tf_op jit(solution)/shard_map/psum | solution.py:55
  426.2 2.6 gather_fusion.9
  432.4 2.3 gather_fusion.8
  436.8 3.8 fusion.105
  440.7 2.0 reshape.105
  444.3 3.6 collective-permute-start.6
  451.3 3.7 collective-permute-done.7
  455.6 2.5 gather_fusion.13
  458.1 2.4 gather_fusion.14
  460.5 2.5 gather_fusion.15
  465.1 1.8 reshape.106
  467.0 2.3 fusion.27
  470.4 1.9 reshape.107
  474.4 1.8 reshape.108
  479.2 2.5 reshape.109
  481.7 3.0 fusion.4
  484.7 1.8 fusion.48
  489.5 53.4 %psum.69 = f32[6,2048]{1,0:T(8,128)S(1)} all-reduce(f32[6,2048]{1,0:T(8,128)S(1)} %bitcast.126), channel_id=1, replica_groups=mesh['space'=32,'scen'=16] {'scen'}, use_global_device_ids=true, to_apply=%region_9.13 | all-reduce | flops 12288 | bytes 98304 | tf_op jit(solution)/shard_map/psum | solution.py:55
  544.2 79.7 %all-reduce.7.cloned.1.call-done = (f32[16,6,2048]{2,0,1:T(8,128)}, f32[4,6,2048]{2,0,1:T(4,128)}) async-done(((f32[16,6,2048]{2,0,1:T(8,128)}, f32[4,6,2048]{2,0,1:T(4,128)}), (f32[16,6,2048]{2,0,1:T(8,128)}, f32[4,6,2048]{2,0,1:T(4,128)})) %all-reduce.7.cloned.1.call-update) | async-done | bytes 983056 | tf_op jit(solution)/shard_map/psum | solution.py:55
  626.7 2.7 gather_fusion.17
  632.4 2.3 gather_fusion.16
  (225 shorter events, 101.8 us)
Async XLA Ops:
  7.2 9.6 %copy-start.40 = (f32[64]{0:T(128)S(1)}, f32[64]{0:T(128)}, u32[]{:S(2)}) copy-start(f32[64]{0:T(128)} %param.19) | copy-start | bytes 772
  7.2 9.7 %copy-start.38 = (s32[2,64]{1,0:T(2,128)S(1)}, s32[2,64]{1,0:T(2,128)}, u32[]{:S(2)}) copy-start(s32[2,64]{1,0:T(2,128)} %param.18) | copy-start | bytes 1540
  7.2 151.4 %all-reduce.11.cloned.1.call-start = ((), (), s32[]{:S(2)}) async-start(), calls=%async_computation.2 | async-start | bytes 1966080 | tf_op jit(solution)/shard_map/psum | solution.py:55
  8.3 68.0 %collective-permute-start = (bf16[4,24,1,512]{3,1,2,0:T(8,128)(2,1)S(1)}, bf16[4,24,1,512]{3,1,2,0:T(8,128)(2,1)S(1)}, u32[]{:S(2)}, u32[]{:S(2)}) collective-permute-start(bf16[4,24,1,512]{3,1,2,0:T(8,128)(2,1)S(1)} %get-tuple-element.41), channel_id=1, source_target_pairs={{0,16},{16,32},{32,48},{48,64},{64,80},{80,96},{96,112},{112,128},... | collective-permute-start | bytes 294920 | tf_op jit(solution)/shard_map/ppermute | solution.py:21
  13.9 62.3 %collective-permute-start.1 = (bf16[4,24,1,512]{3,1,2,0:T(8,128)(2,1)S(1)}, bf16[4,24,1,512]{3,1,2,0:T(8,128)(2,1)S(1)}, u32[]{:S(2)}, u32[]{:S(2)}) collective-permute-start(bf16[4,24,1,512]{3,1,2,0:T(8,128)(2,1)S(1)} %get-tuple-element.40), channel_id=1, source_target_pairs={{16,0},{32,16},{48,32},{64,48},{80,64},{96,80},{112,96},{128,112},... | collective-permute-start | bytes 294920 | tf_op jit(solution)/shard_map/ppermute | solution.py:22
  15.2 4.9 copy-start.39
  15.3 5.1 copy-start.4
  16.9 57.4 %copy-start.26 = (s32[4]{0:T(128)}, s32[4]{0:T(128)S(1)}, u32[]{:S(2)}) copy-start(s32[4]{0:T(128)S(1)} %get-tuple-element.46) | copy-start | bytes 52
  16.9 57.4 %copy-start.28 = (s32[4]{0:T(128)}, s32[4]{0:T(128)S(1)}, u32[]{:S(2)}) copy-start(s32[4]{0:T(128)S(1)} %get-tuple-element.47) | copy-start | bytes 52
  19.4 404.0 %all-reduce.9.cloned.1.call-start = ((), (), s32[]{:S(2)}) async-start(), calls=%async_computation.1 | async-start | bytes 1966080 | tf_op jit(solution)/shard_map/psum | solution.py:55
  20.4 57.6 %copy-start.33 = (pred[4]{0:T(512)(128)(4,1)}, pred[4]{0:T(512)(128)(4,1)S(1)}, u32[]{:S(2)}) copy-start(pred[4]{0:T(512)(128)(4,1)S(1)} %compare_and_fusion.2) | copy-start | bytes 16
  20.5 138.0 %copy-start.36 = (f32[16]{0:T(128)}, f32[16]{0:T(128)S(1)}, u32[]{:S(2)}) copy-start(f32[16]{0:T(128)S(1)} %select_reduce_fusion) | copy-start | bytes 196
  21.2 56.2 %copy-start.24 = (s32[1024]{0:T(1024)}, s32[1024]{0:T(1024)S(1)}, u32[]{:S(2)}) copy-start(s32[1024]{0:T(1024)S(1)} %pad_clamp_fusion.2) | copy-start | bytes 12292
  76.2 3.1 copy-start.25
  158.6 2.8 copy-start.23
  158.6 2.8 copy-start.34
  161.4 9.2 %copy-start.1 = (f32[4,24,2048]{2,1,0:T(8,128)S(1)}, f32[4,24,2048]{2,1,0:T(8,128)}, u32[]{:S(2)}) copy-start(f32[4,24,2048]{2,1,0:T(8,128)} %param.15) | copy-start | bytes 2359300
  161.4 9.2 %copy-start.5 = (bf16[4,24,2048]{2,1,0:T(8,128)(2,1)S(1)}, bf16[4,24,2048]{2,1,0:T(8,128)(2,1)}, u32[]{:S(2)}) copy-start(bf16[4,24,2048]{2,1,0:T(8,128)(2,1)} %param.14) | copy-start | bytes 1179652
  161.4 9.2 %copy-start.14 = (f32[4,6,2048]{2,0,1:T(4,128)S(1)}, f32[4,6,2048]{2,0,1:T(4,128)}, u32[]{:S(2)}) copy-start(f32[4,6,2048]{2,0,1:T(4,128)} %slice.190) | copy-start | bytes 589828
  166.0 8.4 %copy-start.15 = (f32[4,6,2048]{2,0,1:T(4,128)}, f32[4,6,2048]{2,0,1:T(4,128)S(1)}, u32[]{:S(2)}) copy-start(f32[4,6,2048]{2,0,1:T(4,128)S(1)} %copy_select_fusion.4) | copy-start | bytes 589828
  169.6 4.9 copy-start.16
  170.6 3.9 copy-start.17
  176.1 5.3 collective-permute-start.2
  179.8 6.9 %collective-permute-start.3 = (bf16[4,24,1,512]{3,1,2,0:T(8,128)(2,1)S(1)}, bf16[4,24,1,512]{3,1,2,0:T(8,128)(2,1)S(1)}, u32[]{:S(2)}, u32[]{:S(2)}) collective-permute-start(bf16[4,24,1,512]{3,1,2,0:T(8,128)(2,1)S(1)} %copy.232), channel_id=1, source_target_pairs={{16,0},{32,16},{48,32},{64,48},{80,64},{96,80},{112,96},{128,112},... | collective-permute-start | bytes 294920 | tf_op jit(solution)/shard_map/ppermute | solution.py:22
  206.3 3.9 copy-start.29
  217.9 69.0 %collective-permute-start.4 = (bf16[4,24,1,512]{3,1,2,0:T(8,128)(2,1)}, bf16[4,24,1,512]{3,1,2,0:T(8,128)(2,1)}, u32[]{:S(2)}, u32[]{:S(2)}) collective-permute-start(bf16[4,24,1,512]{3,1,2,0:T(8,128)(2,1)} %copy.233), channel_id=1, source_target_pairs={{0,16},{16,32},{32,48},{48,64},{64,80},{80,96},{96,112},{112,128},... | collective-permute-start | bytes 294920 | tf_op jit(solution)/shard_map/ppermute | solution.py:21
  285.3 7.2 %collective-permute-start.5 = (bf16[4,24,1,512]{3,1,2,0:T(8,128)(2,1)}, bf16[4,24,1,512]{3,1,2,0:T(8,128)(2,1)}, u32[]{:S(2)}, u32[]{:S(2)}) collective-permute-start(bf16[4,24,1,512]{3,1,2,0:T(8,128)(2,1)} %copy.234), channel_id=1, source_target_pairs={{16,0},{32,16},{48,32},{64,48},{80,64},{96,80},{112,96},{128,112},... | collective-permute-start | bytes 294920 | tf_op jit(solution)/shard_map/ppermute | solution.py:22
  286.6 337.3 %all-reduce.7.cloned.1.call-start = ((), (), s32[]{:S(2)}) async-start(), calls=%async_computation | async-start | bytes 1966080 | tf_op jit(solution)/shard_map/psum | solution.py:55
  435.9 4.8 copy-start.9
  436.8 3.9 copy-start.11
  442.7 7.6 %copy-start.6 = (bf16[4,24,4,512]{3,2,0,1:T(4,128)(2,1)S(1)}, bf16[4,24,4,512]{3,2,0,1:T(4,128)(2,1)}, u32[]{:S(2)}) copy-start(bf16[4,24,4,512]{3,2,0,1:T(4,128)(2,1)} %reshape.105) | copy-start | bytes 1179652
  444.3 5.3 collective-permute-start.6
  448.1 6.9 %collective-permute-start.7 = (bf16[4,24,1,512]{3,1,2,0:T(8,128)(2,1)S(1)}, bf16[4,24,1,512]{3,1,2,0:T(8,128)(2,1)S(1)}, u32[]{:S(2)}, u32[]{:S(2)}) collective-permute-start(bf16[4,24,1,512]{3,1,2,0:T(8,128)(2,1)S(1)} %copy.236), channel_id=1, source_target_pairs={{16,0},{32,16},{48,32},{64,48},{80,64},{96,80},{112,96},{128,112},... | collective-permute-start | bytes 294920 | tf_op jit(solution)/shard_map/ppermute | solution.py:22
  466.9 2.3 copy-start.22
  479.2 2.5 copy-start.7
  479.2 2.5 copy-start.8
  479.2 2.5 copy-start.10
  479.2 2.5 copy-start.12
  481.7 3.0 copy-start.30
  481.7 4.8 copy-start.27
  484.6 4.4 copy-start.2
  487.6 136.3 %copy-start.37 = (f32[16]{0:T(128)S(1)}, f32[16]{0:T(128)}, u32[]{:S(2)}) copy-start(f32[16]{0:T(128)} %copy-done.36) | copy-start | bytes 196
  625.2 4.2 copy-start.32
  625.2 5.3 copy-start.35
  626.7 8.0 %copy-start.31 = (pred[4]{0:T(512)(128)(4,1)S(1)}, pred[4]{0:T(512)(128)(4,1)}, u32[]{:S(2)}) copy-start(pred[4]{0:T(512)(128)(4,1)} %get-tuple-element.28) | copy-start | bytes 16
  626.7 10.0 %copy-start.3 = (f32[4,24,2048]{2,0,1:T(4,128)S(1)}, f32[4,24,2048]{2,0,1:T(4,128)}, u32[]{:S(2)}) copy-start(f32[4,24,2048]{2,0,1:T(4,128)} %copy-done.2) | copy-start | bytes 2359300
  626.7 10.0 %slice-start = ((f32[4,24,2048]{2,0,1:T(4,128)}), f32[4,6,2048]{2,0,1:T(4,128)S(1)}, s32[]{:S(2)}) async-start(f32[4,24,2048]{2,0,1:T(4,128)} %copy-done.2), calls=%async_computation.3 | async-start | bytes 393216 | tf_op jit(solution)/shard_map/slice | solution.py:34
  626.7 10.0 %copy-start.13 = (f32[4,6,2048]{2,0,1:T(4,128)S(1)}, f32[4,6,2048]{2,0,1:T(4,128)}, u32[]{:S(2)}) copy-start(f32[4,6,2048]{2,0,1:T(4,128)} %copy-done.11) | copy-start | bytes 589828
  (5 other events, 7.2 us)
Sparse Core Ops, SparseCore 0:
  19.6 138.9 all-reduce.10
  286.7 136.6 all-reduce.8
  487.8 136.0 all-reduce.6
where the time goes:
time: 649 us; the launch traced here: 646 us
  waiting for transfers between devices  268 us (41%)
  blocking collectives  160 us (25%)
  local copies, waits for them, and re-layouts  108 us (17%)
  other arithmetic  46.4 us (7%)
  matrix products  25.3 us (4%)
  starting transfers between devices  23.7 us (4%)
  between operations  14.6 us (2%)
    psum x3, waiting for transfers between devices, tree_center(): lax.psum((root_term, first_term, second_term), 'scen')  258 us
    psum x3, blocking collectives, tree_center(): lax.psum((root_term, first_term, second_term), 'scen')  160 us
    gather x12, local copies, waits for them, and re-layouts, descend(): jnp.take(extended, local_cone[:, cone_slot], axis=2).reshape(-1, TILE)  23.2 us
    ppermute x4, starting transfers between devices, extended_2(): before = lax.ppermute(last, axis, up)  17.7 us
    dot_general x12, matrix products, descend(): jnp.dot(picked, patterns[cone_slot], preferred_element_type=jnp.float32)  14.5 us
    reshape x12, local copies, waits for them, and re-layouts, descend(): jnp.take(extended, local_cone[:, cone_slot], axis=2).reshape(-1, TILE)  13.9 us
    unnamed x98, local copies, waits for them, and re-layouts  13.1 us
  transfers between devices with their start and end apart: 11, of which 7 were waited for; matrix products, arithmetic and copies ran while one was open for 9% of the time, Pallas kernels for 0%

commit v1 on v0

v1 whole, which is shorter than its diff:
```python
import functools

import jax
import jax.numpy as jnp
from jax import lax
from jax.experimental import pallas as pl
from jax.experimental.pallas import tpu as pltpu
from jax.sharding import PartitionSpec as P

TILE = 512
ITERS = 2
F32 = jnp.float32
BF16 = jnp.bfloat16
MESH = pl.DeviceIdType.MESH

SCL = 4
PER = 24
ROWS = SCL * PER
TL = 4
CODE = 65534.0
LANES = 128
HALF = 32
MSG = 2 * HALF


def iota(shape, dim):
    return lax.broadcasted_iota(jnp.int32, shape, dim)


def div6(r):
    return (r * 43) >> 8


def div24(r):
    return (r * 171) >> 12


def split(x):
    hi = x.astype(BF16)
    return hi, (x - hi.astype(F32)).astype(BF16)


def encode(x):
    return jnp.round(x * CODE).astype(jnp.int32).astype(jnp.int16)


def decode(v):
    return split(v.astype(jnp.int32).astype(F32))


def dot(a, b):
    return jnp.dot(a, b, preferred_element_type=F32)


def dot_t(a, b):
    return lax.dot_general(a, b, (((1,), (1,)), ((), ())), preferred_element_type=F32)


def kernel(ns, nc, cone, start, ore, dual, pats_hbm, node_row, node_col, prob_row, f_out, d_out,
           rounded, halo, pats, ore_v, f, lin, dacc, cone_acc, sel, expand, weights,
           snd1, rcv1, snd2, rcv2,
           load_sem, out_sem, halo_send, halo_recv, s1_sem, r1_sem, s2_sem, r2_sem):
    sp = lax.axis_index("space")
    sc = lax.axis_index("scen")
    left = lax.rem(sp + ns - 1, ns)
    right = lax.rem(sp + 1, ns)

    def load(k, src, dst):
        return pltpu.make_async_copy(src, dst, load_sem.at[k])

    loads = []
    for t in range(TL):
        loads.append(load(t, start.at[:, pl.ds(t * TILE, TILE)], rounded.at[0, t]))
    loads.append(load(TL, pats_hbm, pats))
    for t in range(TL):
        loads.append(load(TL + 1 + t, dual.at[:, pl.ds(t * TILE, TILE)], dacc.at[t]))
    for t in range(TL):
        loads.append(load(2 * TL + 1 + t, ore.at[:, pl.ds(t * TILE, TILE)], ore_v.at[t]))
    for c in loads:
        c.start()

    barrier = pltpu.get_barrier_semaphore()
    for nb in (left, right):
        pl.semaphore_signal(barrier, inc=1, device_id=(nb, sc), device_id_type=MESH)

    @pl.loop(1, nc)
    def _(d):
        pl.semaphore_signal(barrier, inc=1, device_id=(sp, lax.rem(sc + d, nc)), device_id_type=MESH)

    prob = prob_row[...]
    pn = prob / jnp.sum(prob, axis=1, keepdims=True)
    lane = iota(pn.shape, 1)
    col = iota((MSG, ROWS), 1)
    row = iota((MSG, ROWS), 0)
    cs = div24(col)
    cp = col - PER * cs
    low = row >= HALF
    r = jnp.where(low, row - HALF, row)
    rs = div6(r)
    rq = r - 6 * rs
    section = jnp.where(low, 2, 1)
    picks = (rs < SCL) & (cs == rs) & (cp == 6 * section + rq)
    wcol = jnp.zeros((1, ROWS), F32)
    one_s = div24(iota((1, ROWS), 1))
    for s in range(SCL):
        ps = jnp.sum(jnp.where(lane == sc * SCL + s, pn, 0.0), axis=1, keepdims=True)
        wcol = jnp.where(one_s == s, ps, wcol)
    w_hi = wcol.astype(BF16).astype(F32)
    w_lo = wcol - w_hi
    w_half = jnp.where(low, w_lo, w_hi)
    once = jnp.where(picks, 1.0, jnp.where((rs == SCL) & (cp == rq), w_half, 0.0))
    sel[:, :ROWS] = once.astype(BF16)
    sel[:, ROWS:] = once.astype(BF16)

    er = iota((ROWS, MSG), 0)
    ec = iota((ROWS, MSG), 1)
    es = div24(er)
    ep = er - PER * es
    target = jnp.where(
        ep < 6, 24 + ep, jnp.where(ep < 12, es * 6 + ep - 6, HALF + es * 6 + ep - 12)
    )
    once = jnp.where((ec == target) & (ep < 18), 1.0, 0.0).astype(BF16)
    expand[:, :MSG] = once
    expand[:, MSG:] = once

    rounded[0, TL] = jnp.zeros((ROWS, TILE), BF16)
    row1 = iota((ROWS, 1), 0)
    upper = (row1 - PER * div24(row1)) < 18
    leaf = jnp.where(upper, 0.0, 1.0)
    half_up = jnp.where(upper, 0.5, 0.0)

    def start_halo(step):
        a = pltpu.make_async_remote_copy(
            rounded.at[step, 0], halo.at[step, 1], halo_send.at[step, 0], halo_recv.at[step, 1],
            device_id=(left, sc), device_id_type=MESH)
        b = pltpu.make_async_remote_copy(
            rounded.at[step, TL - 1], halo.at[step, 0], halo_send.at[step, 1], halo_recv.at[step, 0],
            device_id=(right, sc), device_id_type=MESH)
        a.start()
        b.start()
        return a, b

    def send_all(src, dst, s_sem, r_sem, k):
        @pl.loop(1, nc)
        def _(d):
            j = lax.rem(sc + d, nc)
            pltpu.make_async_remote_copy(
                src.at[k, j], dst.at[k, sc], s_sem.at[k], r_sem.at[k],
                device_id=(sp, j), device_id_type=MESH).start()

    def wait_all(buf, sem, k):
        part = buf.at[k, pl.ds(0, nc - 1)]
        pltpu.make_async_copy(part, part, sem.at[k]).wait()

    def pack(k, values):
        for t in range(TL):
            x = jnp.concatenate(split(values(t) - 0.5), axis=0)
            m = dot(sel[...], x)
            top = 4.0 * (m[24:32] + m[56:64])
            m = encode(jnp.concatenate([m[:24], top, m[32:]], axis=0))
            for q in range(TL):
                snd1[k, t * TL + q] = m[:, q * LANES:(q + 1) * LANES]

    def average(k):
        rcv1[k, sc] = snd1[k, sc]
        wait_all(rcv1, r1_sem, k)
        for h in range(2):
            hi, lo = decode(rcv1[k, :, h * HALF:(h + 1) * HALF, :].reshape(nc * HALF, LANES))
            y = dot(weights[h, 0], hi) + (dot(weights[h, 1], hi) + dot(weights[h, 0], lo))
            y = jnp.round(y).astype(jnp.int32).astype(jnp.int16)
            snd2[k, :, h * HALF:(h + 1) * HALF, :] = y.reshape(nc, HALF, LANES)
        send_all(snd2, rcv2, s2_sem, r2_sem, k)
        rcv2[k, sc] = snd2[k, sc]

    def slots(t):
        tile = sp * TL + t
        lid = jnp.maximum(tile - 1, 0)
        a = jnp.where(cone[t, 1] == lid, 1, 2)
        return a, 3 - a

    def cone_own(step):
        own = jnp.concatenate([rounded[step, t] for t in range(TL)], axis=0)
        cone_acc[...] = dot(own, pats[0])
        for k in (1, 2):
            picked = []
            for t in range(TL):
                a, b = slots(t)
                if t == 0:
                    picked.append(jnp.where(b == k, rounded[step, 1], jnp.zeros((), BF16)))
                elif t == TL - 1:
                    picked.append(jnp.where(a == k, rounded[step, TL - 2], jnp.zeros((), BF16)))
                else:
                    picked.append(rounded[step, jnp.where(a == k, t - 1, t + 1)])
            cone_acc[...] += dot(jnp.concatenate(picked, axis=0), pats[k])

    def cone_halo(step, copies):
        for c in copies:
            c.wait()
        a, _ = slots(0)
        lv = jnp.where(sp == 0, rounded[step, 0], halo[step, 0])
        cone_acc[:ROWS] += dot(lv, pats[a])
        _, b = slots(TL - 1)
        rv = jnp.where(sp == ns - 1, rounded[step, TL - 1], halo[step, 1])
        cone_acc[(TL - 1) * ROWS:] += dot(rv, pats[b])

    def chunks(body):
        for t in range(TL):
            for q in range(TILE // LANES):
                body(t, pl.ds(q * LANES, LANES), t * TL + q)

    def center_of(k, j, fv):
        hi, lo = decode(rcv2[k, j])
        c = dot(expand[...], jnp.concatenate([hi, lo], axis=0))
        return c * (1.0 / CODE) + half_up + leaf * fv

    def first_step(it, step):
        def body(t, ln, j):
            if it == 0:
                fv = rounded[0, t, :, ln].astype(F32)
                c = center_of(it, j, fv)
                g = dacc[t, :, ln] - ore_v[t, :, ln].astype(F32) - c
            else:
                fv = f[t, :, ln]
                c = center_of(it, j, fv)
                dv = dacc[t, :, ln] + (fv - c)
                dacc[t, :, ln] = dv
                g = dv - ore_v[t, :, ln].astype(F32) - c
            lin[t, :, ln] = g
            descend(t, ln, fv, g, step)
        chunks(body)

    def second_step(step):
        def body(t, ln, j):
            descend(t, ln, f[t, :, ln], lin[t, :, ln], step)
        chunks(body)

    def descend(t, ln, fv, g, step):
        grad = g + fv + (fv - cone_acc[t * ROWS:(t + 1) * ROWS, ln])
        fv = jnp.clip(fv - 0.4 * grad, 0.0, 1.0)
        f[t, :, ln] = fv
        if step < 3:
            rounded[step + 1, t, :, ln] = fv.astype(BF16)

    for c in loads[:TL]:
        c.wait()
    pack(0, lambda t: rounded[0, t].astype(F32))
    pl.semaphore_wait(barrier, nc + 1)
    send_all(snd1, rcv1, s1_sem, r1_sem, 0)
    copies = start_halo(0)

    n = nc * HALF
    s_of = iota((n, LANES), 0)
    dev, rr = s_of >> 5, s_of & 31
    s6 = div6(rr)
    c = iota((n, LANES), 1)
    for h in range(2):
        same = node_col[:, h:h + 1] == node_row[h:h + 1, :]
        raw = jnp.where(same, prob, 0.0)
        m = raw / jnp.sum(raw, axis=1, keepdims=True)
        m = jnp.concatenate([m, jnp.zeros((64, 64), F32)], axis=1)
        tail = jnp.where((iota((64, LANES), 0) == 0) & (iota((64, LANES), 1) == 64), 0.25, 0.0)
        m = jnp.concatenate([m, tail], axis=0)
        onehot = (s6 < SCL) & (c == dev * SCL + s6)
        if h == 0:
            onehot = onehot | ((s6 == SCL) & (c == 64))
        place = onehot.astype(F32).astype(BF16)
        q_row = iota((1, n), 1) & 31
        q_row = q_row - 6 * div6(q_row)
        for part, mp in enumerate(split(m)):
            for b in range(n // LANES):
                rows = slice(b * LANES, (b + 1) * LANES)
                moved = dot(place[rows], mp).astype(BF16)
                full = dot_t(moved, place)
                q_col = iota((LANES, 1), 0) & 31
                q_col = q_col - 6 * div6(q_col)
                weights[h, part, rows, :] = jnp.where(q_col == q_row, full, 0.0).astype(BF16)

    average(0)
    for c in loads[TL:]:
        c.wait()
    for it in range(ITERS):
        a, b = 2 * it, 2 * it + 1
        cone_own(a)
        cone_halo(a, copies)
        wait_all(rcv2, r2_sem, it)
        first_step(it, a)
        copies = start_halo(b)
        cone_own(b)
        cone_halo(b, copies)
        second_step(b)
        pack(it + 1, lambda t: f[t])
        send_all(snd1, rcv1, s1_sem, r1_sem, it + 1)
        if it + 1 < ITERS:
            copies = start_halo(b + 1)
        average(it + 1)

    outs = []
    for t in range(TL):
        o = pltpu.make_async_copy(f.at[t], f_out.at[:, pl.ds(t * TILE, TILE)], out_sem.at[t])
        o.start()
        outs.append(o)
    wait_all(rcv2, r2_sem, ITERS)

    def finish(t, ln, j):
        lin[t, :, ln] = dacc[t, :, ln] + (f[t, :, ln] - center_of(ITERS, j, f[t, :, ln]))
    for t in range(TL):
        for q in range(TILE // LANES):
            finish(t, pl.ds(q * LANES, LANES), t * TL + q)
        o = pltpu.make_async_copy(lin.at[t], d_out.at[:, pl.ds(t * TILE, TILE)], out_sem.at[TL + t])
        o.start()
        outs.append(o)
    for o in outs:
        o.wait()
    for k in range(ITERS + 1):
        wait_all(snd1, s1_sem, k)
        wait_all(snd2, s2_sem, k)


def body(start_fraction, ore_value, dual_price, patterns, cone_list, node_list, probability):
    ns, nc = lax.axis_size("space"), lax.axis_size("scen")
    blocks = start_fraction.shape[2]
    flat = (ROWS, blocks)
    anyspec = pl.BlockSpec(memory_space=pl.ANY)
    vspec = pl.BlockSpec(memory_space=pltpu.VMEM)
    sspec = pl.BlockSpec(memory_space=pltpu.SMEM)
    steps, avgs = 2 * ITERS, ITERS + 1
    dma = pltpu.SemaphoreType.DMA
    f, d = pl.pallas_call(
        functools.partial(kernel, ns, nc),
        out_shape=[jax.ShapeDtypeStruct(flat, F32)] * 2,
        in_specs=[sspec] + [anyspec] * 4 + [vspec] * 3,
        out_specs=[anyspec] * 2,
        scratch_shapes=[
            pltpu.VMEM((steps, TL + 1, ROWS, TILE), BF16),
            pltpu.VMEM((steps, 2, ROWS, TILE), BF16),
            pltpu.VMEM((3, TILE, TILE), BF16),
            pltpu.VMEM((TL, ROWS, TILE), BF16),
            pltpu.VMEM((TL, ROWS, TILE), F32),
            pltpu.VMEM((TL, ROWS, TILE), F32),
            pltpu.VMEM((TL, ROWS, TILE), F32),
            pltpu.VMEM((TL * ROWS, TILE), F32),
            pltpu.VMEM((MSG, 2 * ROWS), BF16),
            pltpu.VMEM((ROWS, 2 * MSG), BF16),
            pltpu.VMEM((2, 2, nc * HALF, nc * HALF), BF16),
            pltpu.VMEM((avgs, nc, MSG, LANES), jnp.int16),
            pltpu.VMEM((avgs, nc, MSG, LANES), jnp.int16),
            pltpu.VMEM((avgs, nc, MSG, LANES), jnp.int16),
            pltpu.VMEM((avgs, nc, MSG, LANES), jnp.int16),
            dma((3 * TL + 1,)),
            dma((2 * TL,)),
            dma((steps, 2)),
            dma((steps, 2)),
            dma((avgs,)),
            dma((avgs,)),
            dma((avgs,)),
            dma((avgs,)),
        ],
        compiler_params=pltpu.CompilerParams(
            collective_id=0, has_side_effects=True, vmem_limit_bytes=50 * 2**20
        ),
    )(
        cone_list,
        start_fraction.reshape(flat),
        ore_value.reshape(flat),
        dual_price.reshape(flat),
        patterns,
        node_list,
        node_list.T,
        probability.reshape(1, -1),
    )
    return f.reshape(start_fraction.shape), d.reshape(start_fraction.shape)


def solution(mesh):
    in_specs = (
        P("scen", None, "space"),
        P("scen", None, "space"),
        P("scen", None, "space"),
        P(),
        P("space", None),
        P(),
        P(),
    )
    out_specs = (P("scen", None, "space"), P("scen", None, "space"))
    return jax.shard_map(body, mesh=mesh, in_specs=in_specs, out_specs=out_specs, check_vma=False)
```

time: 649 us -> 79.5 us (0.12)
  waiting for transfers between devices: 268 us -> 0 us
  blocking collectives: 160 us -> 0 us
  local copies, waits for them, and re-layouts: 108 us -> 7.67 us
  Pallas kernels: 0 us -> 70.9 us
  other arithmetic: 46.4 us -> 0 us
  matrix products: 25.3 us -> 0 us
  starting transfers between devices: 23.7 us -> 0 us
  between operations: 14.6 us -> 0.64 us
    psum x3 -> x0, waiting for transfers between devices: 258 us -> none  [tree_center(): lax.psum((root_term, first_term, second_term), 'scen')]
    psum x3 -> x0, blocking collectives: 160 us -> none  [tree_center(): lax.psum((root_term, first_term, second_term), 'scen')]
    pallas_call x0 -> x1, Pallas kernels: none -> 70.9 us  [body(): pl.pallas_call(functools.partial(kernel, ns, nc), out_shape=[jax.ShapeDty...]
    gather x18 -> x0, local copies, waits for them, and re-layouts: 38.2 us -> none  [the longest x12 23.2 us: descend(): jnp.take(extended, local_cone[:, cone_slot], axis=2).reshape(-1, TILE)]
    reshape x20 -> x0, local copies, waits for them, and re-layouts: 28.6 us -> none  [the longest x12 13.9 us: descend(): jnp.take(extended, local_cone[:, cone_slot], axis=2).reshape(-1, TILE)]
    dot_general x21 -> x0, matrix products: 25.3 us -> none  [the longest x12 14.5 us: descend(): jnp.dot(picked, patterns[cone_slot], preferred_element_type=jnp.float32)]
    ppermute x8 -> x0, starting transfers between devices: 23.3 us -> none  [the longest x4 17.7 us: extended_2(): before = lax.ppermute(last, axis, up)]
    select_n x20 -> x0, other arithmetic: 16.2 us -> none  [the longest x14 8.87 us: descend(): jnp.take(extended, local_cone[:, cone_slot], axis=2).reshape(-1, TILE)]
  transfers between devices with their start and end apart: 11 -> 0, of which waited for: 7 -> 0; matrix products, arithmetic and copies ran while one was open for 9% -> 0% of each run, Pallas kernels for 0% -> 0%
where the time goes in v1:
time: 79.5 us; the launch traced here: 79.2 us
  Pallas kernels  70.9 us (89%)
  local copies, waits for them, and re-layouts  7.67 us (10%)
    pallas_call x1, Pallas kernels, body(): pl.pallas_call(functools.partial(kernel, ns, nc), out_shape=[jax.ShapeDty...  70.9 us
    unnamed x15, local copies, waits for them, and re-layouts  7.67 us

profile of v1, /device:TPU:1, one launch (start us, length us, event | category | flops | bytes accessed | tf_op | source)
XLA Modules:
  0.0 79.2 jit_solution(13811112089010984382)
XLA Ops:
  0.6 0.8 copy.9
  1.4 0.0 copy-start
  1.4 1.1 %copy-done = f32[4,24,2048]{2,1,0:T(8,128)S(1)} copy-done((f32[4,24,2048]{2,1,0:T(8,128)S(1)}, f32[4,24,2048]{2,1,0:T(8,128)}, u32[]{:S(2)}) %copy-start) | copy-done | bytes 786456
  2.5 0.0 copy-start.1
  2.5 1.0 %copy-done.1 = bf16[4,24,2048]{2,1,0:T(8,128)(2,1)S(1)} copy-done((bf16[4,24,2048]{2,1,0:T(8,128)(2,1)S(1)}, bf16[4,24,2048]{2,1,0:T(8,128)(2,1)}, u32[]{:S(2)}) %copy-start.1) | copy-done | bytes 393240
  3.5 0.0 copy-start.2
  3.5 1.0 %copy-done.2 = bf16[4,24,2048]{2,1,0:T(8,128)(2,1)S(1)} copy-done((bf16[4,24,2048]{2,1,0:T(8,128)(2,1)S(1)}, bf16[4,24,2048]{2,1,0:T(8,128)(2,1)}, u32[]{:S(2)}) %copy-start.2) | copy-done | bytes 393240
  4.5 0.0 copy-start.3
  4.5 0.7 copy-done.3
  5.2 0.0 copy-start.4
  5.2 0.7 copy-done.4
  5.9 0.0 copy-start.5
  5.9 0.7 copy-done.5
  6.5 70.9 %shard_map.86 = (f32[96,2048]{1,0:T(8,128)S(1)}, f32[96,2048]{1,0:T(8,128)S(1)}) custom-call(s32[4,3]{1,0:T(4,128)S(1)} %copy-done.4, bf16[96,2048]{1,0:T(8,128)(2,1)S(1)} %bitcast.10, bf16[96,2048]{1,0:T(8,128)(2,1)S(1)} %bitcast.11, f32[96,2048]{1,0:T(8,128)S(1)} %bitcast.9, bf16[3,512,512]{2,1,0:T(8,128)(2,1)} %pats_hbm.1, s32[2,64]{1,0:T(2,128)S(1)} %copy-done.3, ...), custom_call_target="tpu_custom_call" | custom-call | tf_op jit(solution)/shard_map/pallas_call | solution.py:328
  77.5 0.9 %copy.12 = f32[4,24,2048]{2,1,0:T(8,128)} copy(f32[4,24,2048]{2,1,0:T(8,128)S(1)} %bitcast.8) | data formatting | bytes 1572864
  78.3 0.9 %copy.13 = f32[4,24,2048]{2,1,0:T(8,128)} copy(f32[4,24,2048]{2,1,0:T(8,128)S(1)} %bitcast.7) | data formatting | bytes 1572864
Async XLA Ops:
  1.4 1.1 %copy-start = (f32[4,24,2048]{2,1,0:T(8,128)S(1)}, f32[4,24,2048]{2,1,0:T(8,128)}, u32[]{:S(2)}) copy-start(f32[4,24,2048]{2,1,0:T(8,128)} %param.9) | copy-start | bytes 2359300
  2.5 1.0 %copy-start.1 = (bf16[4,24,2048]{2,1,0:T(8,128)(2,1)S(1)}, bf16[4,24,2048]{2,1,0:T(8,128)(2,1)}, u32[]{:S(2)}) copy-start(bf16[4,24,2048]{2,1,0:T(8,128)(2,1)} %param.7) | copy-start | bytes 1179652
  3.5 1.0 %copy-start.2 = (bf16[4,24,2048]{2,1,0:T(8,128)(2,1)S(1)}, bf16[4,24,2048]{2,1,0:T(8,128)(2,1)}, u32[]{:S(2)}) copy-start(bf16[4,24,2048]{2,1,0:T(8,128)(2,1)} %param.8) | copy-start | bytes 1179652
  4.5 0.7 copy-start.3
  5.2 0.7 copy-start.4
  5.9 0.7 copy-start.5

commit v2 on v0

v2 whole, which is shorter than its diff:
```python
import functools

import jax
import jax.numpy as jnp
from jax import lax
from jax.experimental import pallas as pl
from jax.experimental.pallas import tpu as pltpu
from jax.sharding import PartitionSpec as P

TILE = 512
STEPS = 4
F32 = jnp.float32
BF16 = jnp.bfloat16
I16 = jnp.int16
MESH = pl.DeviceIdType.MESH

SCEN = 64
SCL = 4
PER = 24
HOME = SCL * PER
TL = 4
SEC = 6
UNIT = SCL * SEC
HALF = TILE // 2
MSG = (2 * UNIT, HALF)
ROWS = SCEN * SEC
NCH = 2
CH = ROWS // NCH
SUB = 96
LIN_CODE = 32767.0 / 9.0
FRAC_CODE = 65534.0
GAIN_CODE = 32767.0 / 2.0


def iota(shape, dim):
    return lax.broadcasted_iota(jnp.int32, shape, dim)


def div(r, by, most):
    mul = (1 << 16) // by + 1
    assert all((v * mul) >> 16 == v // by for v in range(most))
    return (r * mul) >> 16


def split(x):
    hi = x.astype(BF16)
    return hi, (x - hi.astype(F32)).astype(BF16)


def to16(x):
    return jnp.round(x).astype(jnp.int32).astype(I16)


def from16(v):
    return v.astype(jnp.int32).astype(F32)


def dot(a, b):
    return jnp.dot(a, b, preferred_element_type=F32)


def dot_t(a, b):
    return lax.dot_general(a, b, (((1,), (1,)), ((), ())), preferred_element_type=F32)


def fold(x):
    return jnp.concatenate([x[:, :HALF], x[:, HALF:]], axis=0)


def kernel(ns, nc, cone_in, node_in, prob_in, start, ore, dual, pats_in, f_out, d_out,
           cone, node, prob_v, f0_v, ore_v, dual_v, pats, perm, back, mean,
           rounded, halo, f, low, lin, gain, cone_acc,
           snd_f, rcv_f, snd_l, rcv_l, snd_o, rcv_o, snd_d, rcv_d, out_f, out_d,
           load_sem, out_sem, halo_send, halo_recv, a_send, a_recv, b_send):
    sp = lax.axis_index("space")
    sc = lax.axis_index("scen")
    x = lax.div(sc, TL)
    t_own = lax.rem(sc, TL)
    first = t_own == 0
    last = t_own == TL - 1
    left = (jnp.where(first, lax.rem(sp + ns - 1, ns), sp), jnp.where(first, sc + TL - 1, sc - 1))
    right = (jnp.where(last, lax.rem(sp + 1, ns), sp), jnp.where(last, sc - (TL - 1), sc + 1))

    barrier = pltpu.get_barrier_semaphore()
    for nb in (left, right):
        pl.semaphore_signal(barrier, inc=1, device_id=nb, device_id_type=MESH)

    @pl.loop(1, nc)
    def _(d):
        pl.semaphore_signal(barrier, inc=1, device_id=(sp, lax.rem(sc + d, nc)), device_id_type=MESH)

    def load(k, src, dst):
        c = pltpu.make_async_copy(src, dst, load_sem.at[k])
        c.start()
        return c

    load_f0 = load(0, start, f0_v)
    load_ore = load(1, ore, ore_v)
    load_dual = load(2, dual, dual_v)
    load_node = load(3, node_in, node)
    load_prob = load(4, prob_in, prob_v)
    load_cone = load(5, cone_in, cone)
    load_pats = load(6, pats_in, pats)

    def places(shape, home_dim):
        h, g = iota(shape, home_dim), iota(shape, 1 - home_dim)
        hs = div(h, PER, HOME)
        hp = h - PER * hs
        hx = div(hp, SEC, PER)
        return (hx * UNIT + hs * SEC + (hp - SEC * hx)) == g

    perm[...] = jnp.where(places((HOME, HOME), 1), 1.0, 0.0).astype(BF16)
    back[...] = jnp.where(places((HOME, HOME), 0), 1.0, 0.0).astype(BF16)

    def send_all(src, dst, k):
        @pl.loop(1, nc)
        def _(d):
            j = lax.rem(sc + d, nc)
            pltpu.make_async_remote_copy(
                src.at[j], dst.at[sc], a_send.at[k], a_recv.at[k],
                device_id=(sp, j), device_id_type=MESH).start()

    def wait_all(buf, sem, k):
        part = buf.at[pl.ds(0, nc - 1)]
        pltpu.make_async_copy(part, part, sem.at[k]).wait()

    load_f0.wait()
    for t in range(TL):
        m = dot(perm[...], f0_v[:, t * TILE:(t + 1) * TILE])
        for g in range(nc // TL):
            snd_f[g * TL + t] = fold(m[g * UNIT:(g + 1) * UNIT]).astype(BF16)
    pl.semaphore_wait(barrier, nc + 1)
    send_all(snd_f, rcv_f, 0)
    rcv_f[sc] = snd_f[sc]

    load_ore.wait()
    load_dual.wait()
    for t in range(TL):
        ln = slice(t * TILE, (t + 1) * TILE)
        v = jnp.round((dual_v[:, ln] - ore_v[:, ln].astype(F32)) * LIN_CODE)
        hi, lo = split(v)
        m = dot(perm[...], hi) + dot(perm[...], lo)
        for g in range(nc // TL):
            snd_l[g * TL + t] = to16(fold(m[g * UNIT:(g + 1) * UNIT]))
    send_all(snd_l, rcv_l, 1)
    rcv_l[sc] = snd_l[sc]

    load_node.wait()
    load_prob.wait()
    prob = prob_v[...]
    nodes = jnp.where(x == 2, node[1:2, :], node[0:1, :])
    onehot = jnp.where(iota((16, SCEN), 0) == nodes, 1.0, 0.0)
    same = lax.dot_general(onehot.T.astype(BF16), onehot.astype(BF16), (((1,), (0,)), ((), ())),
                           preferred_element_type=F32)
    eye = jnp.where(iota((SCEN, SCEN), 0) == iota((SCEN, SCEN), 1), 1.0, 0.0)
    same = jnp.where(x == 0, jnp.ones_like(same), jnp.where(x == 3, eye, same))
    raw = same * prob
    m = raw / jnp.sum(raw, axis=1, keepdims=True)
    r = iota((ROWS, SCEN), 0)
    of = jnp.where(div(r, SEC, ROWS) == iota((ROWS, SCEN), 1), 1.0, 0.0).astype(BF16)
    rc = iota((ROWS, 1), 0)
    rr = iota((1, ROWS), 1)
    p_col = rc - SEC * div(rc, SEC, ROWS)
    p_row = rr - SEC * div(rr, SEC, ROWS)
    for k, part in enumerate(split(m)):
        moved = dot(of, part).astype(BF16)
        for b in range(ROWS // SUB):
            rows = slice(b * SUB, (b + 1) * SUB)
            full = dot_t(moved[rows], of)
            mean[k, rows, :] = jnp.where(p_col[rows] == p_row, full, 0.0).astype(BF16)

    def pieces(rows0, rows1):
        for r0 in range(rows0, rows1, SUB):
            for q in range(TILE // 128):
                yield slice(r0, r0 + SUB), slice(q * 128, (q + 1) * 128)

    def start_halo(step, c):
        rows = pl.ds(c * CH, CH)
        for side, nb in ((1, left), (0, right)):
            pltpu.make_async_remote_copy(
                rounded.at[step, rows], halo.at[step, side, rows],
                halo_send.at[step, side], halo_recv.at[step, side, c],
                device_id=nb, device_id_type=MESH).start()

    def wait_halo(step, c):
        for side in (0, 1):
            part = halo.at[step, side, pl.ds(c * CH, CH)]
            pltpu.make_async_copy(part, part, halo_recv.at[step, side, c]).wait()

    wait_all(rcv_f, a_recv, 0)
    for i in range(nc):
        v = rcv_f[i].astype(F32)
        rows = slice(i * UNIT, (i + 1) * UNIT)
        f[rows, :HALF] = v[:UNIT]
        f[rows, HALF:] = v[UNIT:]
    for c in range(NCH):
        for rows, ln in pieces(c * CH, (c + 1) * CH):
            rounded[0, rows, ln] = f[rows, ln].astype(BF16)
        start_halo(0, c)

    load_cone.wait()
    load_pats.wait()
    tile = sp * TL + t_own
    slot = jnp.where(cone[t_own, 1] == jnp.maximum(tile - 1, 0), 1, 2)
    at_left = tile == 0
    at_right = tile == ns * TL - 1

    def average(step):
        hi = rounded[step]
        c = dot(mean[0], hi) + dot(mean[1], hi)
        return c if step == 0 else c + dot(mean[0], low[...])

    cen = average(0)
    gain[...] = cen
    cone_acc[...] = dot(rounded[0], pats[0])
    wait_all(rcv_l, a_recv, 1)
    for i in range(nc):
        v = from16(rcv_l[i]) * (1.0 / LIN_CODE)
        rows = slice(i * UNIT, (i + 1) * UNIT)
        lin[rows, :HALF] = v[:UNIT] - gain[rows, :HALF]
        lin[rows, HALF:] = v[UNIT:] - gain[rows, HALF:]

    def step(s):
        for c in range(NCH):
            wait_halo(s, c)
            rc = slice(c * CH, (c + 1) * CH)
            lv = jnp.where(at_left, rounded[s, rc], halo[s, 0, rc])
            rv = jnp.where(at_right, rounded[s, rc], halo[s, 1, rc])
            cone_acc[rc] += dot(lv, pats[slot]) + dot(rv, pats[3 - slot])
            for rows, ln in pieces(c * CH, (c + 1) * CH):
                fv = f[rows, ln]
                grad = lin[rows, ln] + fv + (fv - cone_acc[rows, ln])
                fv = jnp.clip(fv - 0.4 * grad, 0.0, 1.0)
                f[rows, ln] = fv
                if s < STEPS - 1 or s % 2:
                    hi = fv.astype(BF16)
                    rounded[s + 1, rows, ln] = hi
                    if s % 2:
                        low[rows, ln] = (fv - hi.astype(F32)).astype(BF16)
            if s < STEPS - 1:
                start_halo(s + 1, c)
            else:
                for i in range(c * nc // NCH, (c + 1) * nc // NCH):
                    snd_o[i] = to16(fold((f[i * UNIT:(i + 1) * UNIT] - 0.5) * FRAC_CODE))
        if s < STEPS - 1:
            cone_acc[...] = dot(rounded[s + 1], pats[0])

    step(0)
    step(1)
    cen = average(2)
    gain[...] = f[...] - cen
    lin[...] = lin_next(lin, gain, cen, rcv_l, nc)
    step(2)
    step(3)
    send_all(snd_o, rcv_o, 2)
    rcv_o[sc] = snd_o[sc]
    cen = average(4)
    gain[...] += f[...] - cen
    for i in range(nc):
        snd_d[i] = to16(fold(gain[i * UNIT:(i + 1) * UNIT] * GAIN_CODE))
    send_all(snd_d, rcv_d, 3)
    rcv_d[sc] = snd_d[sc]

    def home(rcv, t):
        v = jnp.concatenate([from16(rcv[g * TL + t]) for g in range(nc // TL)], axis=0)
        parts = []
        for h in range(2):
            half = jnp.concatenate(
                [v[(2 * g + h) * UNIT:(2 * g + h + 1) * UNIT] for g in range(nc // TL)], axis=0)
            hi, lo = split(half)
            parts.append(dot(back[...], hi) + dot(back[...], lo))
        return jnp.concatenate(parts, axis=1)

    outs = []
    wait_all(rcv_o, a_recv, 2)
    for t in range(TL):
        ln = slice(t * TILE, (t + 1) * TILE)
        out_f[:, ln] = home(rcv_o, t) * (1.0 / FRAC_CODE) + 0.5
    outs.append(pltpu.make_async_copy(out_f, f_out, out_sem.at[0]))
    outs[-1].start()
    wait_all(rcv_d, a_recv, 3)
    for t in range(TL):
        ln = slice(t * TILE, (t + 1) * TILE)
        out_d[:, ln] = dual_v[:, ln] + home(rcv_d, t) * (1.0 / GAIN_CODE)
    outs.append(pltpu.make_async_copy(out_d, d_out, out_sem.at[1]))
    outs[-1].start()
    for o in outs:
        o.wait()
    for k, buf in enumerate((snd_f, snd_l, snd_o, snd_d)):
        wait_all(buf, a_send, k)
    for s in range(STEPS):
        for side in range(2):
            part = halo.at[s, side]
            pltpu.make_async_copy(part, part, halo_send.at[s, side]).wait()


def lin_next(lin, gain, cen, rcv_l, nc):
    v = [from16(rcv_l[i]) * (1.0 / LIN_CODE) for i in range(nc)]
    v = jnp.concatenate([jnp.concatenate([u[:UNIT], u[UNIT:]], axis=1) for u in v], axis=0)
    return v + gain[...] - cen


def body(start_fraction, ore_value, dual_price, patterns, cone_list, node_list, probability):
    ns, nc = lax.axis_size("space"), lax.axis_size("scen")
    blocks = start_fraction.shape[2]
    flat = (HOME, blocks)
    hbm = pl.BlockSpec(memory_space=pltpu.HBM)
    dma = pltpu.SemaphoreType.DMA
    v = pltpu.VMEM
    f, d = pl.pallas_call(
        functools.partial(kernel, ns, nc),
        out_shape=[jax.ShapeDtypeStruct(flat, F32)] * 2,
        in_specs=[hbm] * 7,
        out_specs=[hbm] * 2,
        scratch_shapes=[
            pltpu.SMEM((TL, 3), jnp.int32),
            v((2, SCEN), jnp.int32),
            v((1, SCEN), F32),
            v(flat, BF16),
            v(flat, BF16),
            v(flat, F32),
            v((3, TILE, TILE), BF16),
            v((HOME, HOME), BF16),
            v((HOME, HOME), BF16),
            v((2, ROWS, ROWS), BF16),
            v((STEPS + 1, ROWS, TILE), BF16),
            v((STEPS, 2, ROWS, TILE), BF16),
            v((ROWS, TILE), F32),
            v((ROWS, TILE), BF16),
            v((ROWS, TILE), F32),
            v((ROWS, TILE), F32),
            v((ROWS, TILE), F32),
            v((nc, *MSG), BF16),
            v((nc, *MSG), BF16),
            v((nc, *MSG), I16),
            v((nc, *MSG), I16),
            v((nc, *MSG), I16),
            v((nc, *MSG), I16),
            v((nc, *MSG), I16),
            v((nc, *MSG), I16),
            v(flat, F32),
            v(flat, F32),
            dma((7,)),
            dma((2,)),
            dma((STEPS, 2)),
            dma((STEPS, 2, NCH)),
            dma((4,)),
            dma((4,)),
            dma((1,)),
        ],
        compiler_params=pltpu.CompilerParams(
            collective_id=0, has_side_effects=True, vmem_limit_bytes=56 * 2**20
        ),
    )(
        cone_list,
        node_list,
        probability.reshape(1, -1),
        start_fraction.reshape(flat),
        ore_value.reshape(flat),
        dual_price.reshape(flat),
        patterns,
    )
    return f.reshape(start_fraction.shape), d.reshape(start_fraction.shape)


def solution(mesh):
    in_specs = (
        P("scen", None, "space"),
        P("scen", None, "space"),
        P("scen", None, "space"),
        P(),
        P("space", None),
        P(),
        P(),
    )
    out_specs = (P("scen", None, "space"), P("scen", None, "space"))
    return jax.shard_map(body, mesh=mesh, in_specs=in_specs, out_specs=out_specs, check_vma=False)
```

time: 649 us -> 61.1 us (0.09)
  waiting for transfers between devices: 268 us -> 0 us
  blocking collectives: 160 us -> 0 us
  local copies, waits for them, and re-layouts: 108 us -> 3.02 us
  Pallas kernels: 0 us -> 57.2 us
  other arithmetic: 46.4 us -> 0 us
  matrix products: 25.3 us -> 0 us
  starting transfers between devices: 23.7 us -> 0 us
  between operations: 14.6 us -> 0.65 us
    psum x3 -> x0, waiting for transfers between devices: 258 us -> none  [tree_center(): lax.psum((root_term, first_term, second_term), 'scen')]
    psum x3 -> x0, blocking collectives: 160 us -> none  [tree_center(): lax.psum((root_term, first_term, second_term), 'scen')]
    pallas_call x0 -> x1, Pallas kernels: none -> 57.2 us  [body(): pl.pallas_call(functools.partial(kernel, ns, nc), out_shape=[jax.ShapeDty...]
    gather x18 -> x0, local copies, waits for them, and re-layouts: 38.2 us -> none  [the longest x12 23.2 us: descend(): jnp.take(extended, local_cone[:, cone_slot], axis=2).reshape(-1, TILE)]
    reshape x20 -> x0, local copies, waits for them, and re-layouts: 28.6 us -> none  [the longest x12 13.9 us: descend(): jnp.take(extended, local_cone[:, cone_slot], axis=2).reshape(-1, TILE)]
    dot_general x21 -> x0, matrix products: 25.3 us -> none  [the longest x12 14.5 us: descend(): jnp.dot(picked, patterns[cone_slot], preferred_element_type=jnp.float32)]
    ppermute x8 -> x0, starting transfers between devices: 23.3 us -> none  [the longest x4 17.7 us: extended_2(): before = lax.ppermute(last, axis, up)]
    select_n x20 -> x0, other arithmetic: 16.2 us -> none  [the longest x14 8.87 us: descend(): jnp.take(extended, local_cone[:, cone_slot], axis=2).reshape(-1, TILE)]
  transfers between devices with their start and end apart: 11 -> 0, of which waited for: 7 -> 0; matrix products, arithmetic and copies ran while one was open for 9% -> 0% of each run, Pallas kernels for 0% -> 0%
where the time goes in v2:
time: 61.1 us; the launch traced here: 60.9 us
  Pallas kernels  57.2 us (94%)
  local copies, waits for them, and re-layouts  3.02 us (5%)
  between operations  0.65 us (1%)
    pallas_call x1, Pallas kernels, body(): pl.pallas_call(functools.partial(kernel, ns, nc), out_shape=[jax.ShapeDty...  57.2 us
    unnamed x4, local copies, waits for them, and re-layouts  3.02 us

profile of v2, /device:TPU:1, one launch (start us, length us, event | category | flops | bytes accessed | tf_op | source)
XLA Modules:
  0.0 60.9 jit_solution(3842868384485132256)
XLA Ops:
  0.6 57.2 %shard_map.86 = (f32[96,2048]{1,0:T(8,128)}, f32[96,2048]{1,0:T(8,128)}) custom-call(s32[4,3]{1,0:T(4,128)} %cone_in.1, s32[2,64]{1,0:T(2,128)} %node_in.1, f32[1,64]{1,0:T(1,128)} %bitcast.11, bf16[96,2048]{1,0:T(8,128)(2,1)} %bitcast.9, bf16[96,2048]{1,0:T(8,128)(2,1)} %bitcast.10, f32[96,2048]{1,0:T(8,128)} %bitcast.8, bf16[3,512,512]{2,1,0:T(8,128)(2,1)} %pats_in.1), custom_call_target="tpu_custom_call" | custom-call | tf_op jit(solution)/shard_map/pallas_call | solution.py:310
  57.9 0.0 copy-start
  57.9 2.1 %copy.11 = f32[4,24,2048]{2,1,0:T(8,128)} copy(f32[4,24,2048]{2,1,0:T(8,128)} %bitcast.7) | data formatting | bytes 1572864
  60.0 0.0 copy-done
  60.0 0.9 %copy.12 = f32[4,24,2048]{2,1,0:T(8,128)} copy(f32[4,24,2048]{2,1,0:T(8,128)S(1)} %bitcast.6) | data formatting | bytes 1572864
Async XLA Ops:
  57.9 2.1 %copy-start = (f32[96,2048]{1,0:T(8,128)S(1)}, f32[96,2048]{1,0:T(8,128)}, u32[]{:S(2)}) copy-start(f32[96,2048]{1,0:T(8,128)} %get-tuple-element.5) | copy-start | bytes 2359300

commit v3 on v0

v3 whole, which is shorter than its diff:
```python
import functools

import jax
import jax.numpy as jnp
from jax import lax
from jax.experimental import pallas as pl
from jax.experimental.pallas import tpu as pltpu
from jax.sharding import PartitionSpec as P

TILE = 512
STEPS = 4
F32 = jnp.float32
BF16 = jnp.bfloat16
I16 = jnp.int16
MESH = pl.DeviceIdType.MESH

SCEN = 64
SCL = 4
PER = 24
HOME = SCL * PER
TL = 4
GRP = 3
HALF = TILE // 2
MAIN, EXTRA = 4, 2
UNITS = MAIN + EXTRA
RUNS = ((0, MAIN), (MAIN, UNITS))
ROWS = MAIN * SCL
LIN_CODE = 32767.0 / 9.0
FRAC_CODE = 65534.0
GAIN_CODE = 32767.0 / 2.0


def iota(shape, dim):
    return lax.broadcasted_iota(jnp.int32, shape, dim)


def div(r, by, most):
    mul = (1 << 16) // by + 1
    assert all((v * mul) >> 16 == v // by for v in range(most))
    return (r * mul) >> 16


def split(x):
    hi = x.astype(BF16)
    return hi, (x - hi.astype(F32)).astype(BF16)


def round16(x):
    return jnp.round(x).astype(jnp.int32)


def wide(v):
    return v.astype(F32) if v.dtype == BF16 else v.astype(jnp.int32).astype(F32)


def dot(a, b):
    return jnp.dot(a, b, preferred_element_type=F32)


def dot_0(a, b):
    return lax.dot_general(a, b, (((0,), (0,)), ((), ())), preferred_element_type=F32)


def fold(x):
    return jnp.concatenate([x[:, :HALF], x[:, HALF:]], axis=0)


def unfold(x):
    h = ROWS // 2
    return jnp.concatenate([x[:h], x[h:]], axis=1)


def kernel(ns, nc, cone_in, node_in, prob_in, start, ore, dual, pats_in, out_f, out_d,
           cone, node, prob_v, f0_v, ore_v, dual_v, pats, perm, back, order, mean,
           rounded, halo, f, low, lin, gain, cone_acc,
           snd_f, rcv_f, snd_l, rcv_l, snd_o, rcv_o, snd_d, rcv_d,
           snd_fe, rcv_fe, snd_le, rcv_le, snd_oe, rcv_oe, snd_de, rcv_de, cone_v,
           load_sem, halo_send, halo_recv, a_send, a_recv, cone_sem):
    sp = lax.axis_index("space")
    sc = lax.axis_index("scen")
    z, yh = lax.div(sp, 2), lax.rem(sp, 2)
    x, yl, core = lax.div(sc, 4), lax.rem(lax.div(sc, 2), 2), lax.rem(sc, 2)
    odd = lax.rem(z, 2)
    half = lax.rem(yl + odd, 2)
    y_own = lax.rem(yh + odd, 2)
    main_slot = (2 * x + yh) * 2 + yl
    extra_slot = (2 * x + yh) * 2 + core
    main_home = core == yh
    extra_home = half == yh
    near = (sp, sc + 1 - 2 * core)
    over = (jnp.where(core == 0, lax.rem(sp + ns - 2, ns), lax.rem(sp + 2, ns)), near[1])
    inside = half != core
    far = (over, (jnp.where(inside, sp, over[0]), jnp.where(inside, 4 * x + 2 * (1 - yl) + 1 - core, over[1])))

    barrier = pltpu.get_barrier_semaphore()
    for nb in (near, over):
        pl.semaphore_signal(barrier, inc=1, device_id=nb, device_id_type=MESH)

    @pl.loop(1, 2 * nc)
    def _(d):
        k = lax.rem(yh * nc + sc + d, 2 * nc)
        pl.semaphore_signal(barrier, inc=1, device_id=(2 * z + lax.div(k, nc), lax.rem(k, nc)), device_id_type=MESH)

    def load(k, src, dst):
        c = pltpu.make_async_copy(src, dst, load_sem.at[k])
        c.start()
        return c

    load_f0 = load(0, start, f0_v)
    load_ore = load(1, ore, ore_v)
    load_dual = load(2, dual, dual_v)
    load_node = load(3, node_in, node)
    load_prob = load(4, prob_in, prob_v)
    load_cone = load(5, cone_in, cone_v.at[0])
    load_pats = load(6, pats_in, pats)

    def places(home_dim):
        n = TL * HOME
        shape = (n, n)
        h, g = iota(shape, home_dim), iota(shape, 1 - home_dim)
        if home_dim:
            h1 = iota((1, n), 1)
        else:
            h1 = iota((n, 1), 0)
        tile = div(h1, HOME, n)
        hr = h1 - HOME * tile
        hs = div(hr, PER, HOME)
        hp = hr - PER * hs
        hg = div(hp, GRP, PER)
        which = hp - GRP * hg
        at_main = (hg * 2 + (which >> 1)) * ROWS + tile * SCL + hs
        at_extra = nc * ROWS + hg * ROWS + tile * SCL + hs
        return jnp.where(jnp.where(which == 1, at_extra, at_main) == g, 1.0, 0.0).astype(BF16)

    perm[...] = places(1)
    back[...] = places(0)

    n = SCEN * MAIN
    q, g = iota((n, 1), 0), iota((1, n), 1)
    order_m = jnp.where(
        ((q & (SCEN - 1)) >> 2) * ROWS + (q >> 6) * SCL + (q & 3) == g, 1.0, 0.0).astype(BF16)
    q, g = iota((n // 2, 1), 0), iota((1, n // 2), 1)
    order_e = jnp.where(
        ((q & (SCEN - 1)) >> 2) * (ROWS // 2) + (q >> 6) * SCL + (q & 3) == g, 1.0, 0.0).astype(BF16)

    bufs = (
        ((snd_f, rcv_f), (snd_fe, rcv_fe)),
        ((snd_l, rcv_l), (snd_le, rcv_le)),
        ((snd_o, rcv_o), (snd_oe, rcv_oe)),
        ((snd_d, rcv_d), (snd_de, rcv_de)),
    )

    def send(skip, own, src, dst, mine, k, device):
        @pl.loop(0, nc)
        def _(d):
            m = lax.rem(own + 1 + d, nc)

            @pl.when(jnp.logical_not(skip & (m == own)))
            def _():
                pltpu.make_async_remote_copy(
                    src.at[m], dst.at[mine], a_send.at[k], a_recv.at[k],
                    device_id=device(m), device_id_type=MESH).start()

        @pl.when(skip)
        def _():
            dst[mine] = src[own]

    def main_owner(m):
        g = lax.div(m, 2)
        return 2 * z + lax.rem(g, 2), 4 * lax.div(g, 2) + 2 * lax.rem(m, 2) + yh

    def extra_owner(m):
        g = lax.div(m, 2)
        return 2 * z + lax.rem(g, 2), 4 * lax.div(g, 2) + 2 * y_own + lax.rem(m, 2)

    def send_out(k, e):
        if e:
            send(extra_home, extra_slot, *bufs[k][1], sc, 2 * k + 1, extra_owner)
        else:
            send(main_home, main_slot, *bufs[k][0], sc, 2 * k, main_owner)

    def send_back(k, e):
        if e:
            send(extra_home, sc, *bufs[k][1], extra_slot, 2 * k + 1, lambda i: (2 * z + half, i))
        else:
            send(main_home, sc, *bufs[k][0], main_slot, 2 * k, lambda i: (2 * z + core, i))

    def wait_all(k, e, sem, buf):
        kept = (main_home, extra_home)[e]

        @pl.when(kept)
        def _():
            part = buf.at[pl.ds(0, nc - 1)]
            pltpu.make_async_copy(part, part, sem.at[2 * k + e]).wait()

        @pl.when(jnp.logical_not(kept))
        def _():
            pltpu.make_async_copy(buf, buf, sem.at[2 * k + e]).wait()

    def pack(snd, snd_e, terms, encode):
        m = encode(sum(dot(perm[...], term) for term in terms))
        n = nc * ROWS
        snd[...] = m[:n].astype(snd.dtype).reshape(nc, ROWS, TILE)
        for j in range(nc):
            snd_e[j] = fold(m[n + 8 * j:n + 8 * j + 8]).astype(snd.dtype)

    def tiles(fn):
        return jnp.concatenate([fn(slice(t * TILE, (t + 1) * TILE)) for t in range(TL)], axis=0)

    load_f0.wait()
    pack(snd_f, snd_fe, [tiles(lambda ln: f0_v[:, ln])], lambda v: v)
    load_ore.wait()
    load_dual.wait()

    lin_home = tiles(lambda ln: jnp.round((dual_v[:, ln] - ore_v[:, ln].astype(F32)) * LIN_CODE))
    pack(snd_l, snd_le, split(lin_home), round16)
    load_node.wait()
    load_prob.wait()
    prob = prob_v[...]
    nodes = jnp.where(x == 2, node[1:2, :], node[0:1, :])
    onehot = jnp.where(iota((16, SCEN), 0) == nodes, 1.0, 0.0)
    same = lax.dot_general(onehot.T.astype(BF16), onehot.astype(BF16), (((1,), (0,)), ((), ())),
                           preferred_element_type=F32)
    eye = jnp.where(iota((SCEN, SCEN), 0) == iota((SCEN, SCEN), 1), 1.0, 0.0)
    same = jnp.where(x == 0, jnp.ones_like(same), jnp.where(x == 3, eye, same))
    raw = same * prob
    m = raw / jnp.sum(raw, axis=1, keepdims=True)
    for k, part in enumerate(split(m)):
        mean[k] = part
    for s in range(STEPS):
        rounded[s, UNITS] = jnp.zeros((SCEN, TILE), BF16)
    order[...] = order_m

    pl.semaphore_wait(barrier, 2 * nc + 1)
    for e in (1, 0):
        for k in range(2):
            send_out(k, e)
    load_cone.wait()
    cone_copy = pltpu.make_async_remote_copy(
        cone_v.at[0], cone_v.at[1], cone_sem.at[0], cone_sem.at[1],
        device_id=(2 * z + 1 - yh, sc), device_id_type=MESH)
    cone_copy.start()

    def start_halo(step, e, u, side, to):
        pltpu.make_async_remote_copy(
            rounded.at[step, u], halo.at[step, e, 1 - side],
            halo_send.at[step, e, side], halo_recv.at[step, e, 1 - side],
            device_id=to, device_id_type=MESH).start()

    ends = [(e, core, (MAIN + core if e else (MAIN - 1) * core), far[e]) for e in range(2)]
    ends += [(e, 1 - core, (MAIN + 1 - core if e else (MAIN - 1) * (1 - core)), near) for e in range(2)]

    ends = [[end for end in ends[2:] + ends[:2] if end[0] == e] for e in range(2)]

    def received(k, e):
        wait_all(k, e, a_recv, bufs[k][e][1])
        rcv = bufs[k][e][1]
        if e:
            v = jnp.concatenate([unfold(wide(rcv[i])) for i in range(nc)], axis=0)
        else:
            v = wide(rcv[...].reshape(nc * ROWS, TILE))
        terms = split(v) if k else (v.astype(BF16),)
        v = sum(dot(order_e if e else order[...], term) for term in terms)
        first, last = RUNS[e]
        return {u: v[(u - first) * SCEN:(u - first + 1) * SCEN] for u in range(first, last)}

    def take_fraction(e):
        for u, fv in received(0, e).items():
            f[u] = fv
            rounded[0, u] = fv.astype(BF16)
        for _, side, u, to in ends[e][::-1]:
            start_halo(0, e, u, side, to)

    take_fraction(1)
    cone_copy.wait()
    cone_loads = [pltpu.make_async_copy(cone_v.at[k], cone.at[k], cone_sem.at[2 + k]) for k in range(2)]
    for c in cone_loads:
        c.start()
    for c in cone_loads:
        c.wait()
    load_pats.wait()
    tile, lslot = [], []
    for u in range(UNITS):
        run, at = (core, u) if u < MAIN else (half, 2 * core + u - MAIN)
        tile.append((2 * z + run) * TL + at)
        lslot.append(jnp.where(cone[jnp.where(run == yh, 0, 1), at, 1] == jnp.maximum(tile[u] - 1, 0), 1, 2))

    def average(step, u):
        hi = rounded[step, u]
        c = dot(mean[0], hi) + dot(mean[1], hi)
        return c if step == 0 else c + dot(mean[0], low[u])

    def cone_own(e, step):
        first, last = RUNS[e]
        n = last - first
        acc = dot(rounded[step, first:last].reshape(n * SCEN, TILE), pats[0])
        for k in (1, 2):
            picked = []
            for u in range(first, last):
                to_left = UNITS if u == first else u - 1
                to_right = UNITS if u == last - 1 else u + 1
                picked.append(rounded[step, jnp.where(lslot[u] == k, to_left, to_right)])
            acc = acc + dot(jnp.concatenate(picked, axis=0), pats[k])
        cone_acc[first:last] = acc.reshape(n, SCEN, TILE)

    def first_center(e):
        for u in range(*RUNS[e]):
            gain[u] = average(0, u)
        cone_own(e, 0)

    def take_linear(e):
        for u, lv in received(1, e).items():
            lin[u] = lv * (1.0 / LIN_CODE) - gain[u]

    def descend(s, u):
        for q in range(TILE // 128):
            ln = slice(q * 128, (q + 1) * 128)
            fv = f[u, :, ln]
            grad = lin[u, :, ln] + fv + (fv - cone_acc[u, :, ln])
            fv = jnp.clip(fv - 0.4 * grad, 0.0, 1.0)
            f[u, :, ln] = fv
            hi = fv.astype(BF16)
            rounded[s + 1, u, :, ln] = hi
            if s % 2:
                low[u, :, ln] = (fv - hi.astype(F32)).astype(BF16)

    def step(e, s):
        first, last = RUNS[e]
        for u in range(first + 1, last - 1):
            descend(s, u)
        for _, side, u, to in ends[e]:
            here = halo.at[s, e, side]
            pltpu.make_async_copy(here, here, halo_recv.at[s, e, side]).wait()
            at_end = jnp.where(side == 0, tile[first] == 0, tile[last - 1] == ns * TL - 1)
            slot = jnp.where(side == 0, lslot[first], 3 - lslot[last - 1])
            away = jnp.where(at_end, rounded[s, u], halo[s, e, side])
            cone_acc[u] += dot(away, pats[slot])
            descend(s, u)
            if s < STEPS - 1:
                start_halo(s + 1, e, u, side, to)
        if s < STEPS - 1:
            cone_own(e, s + 1)
        if s == 1:
            for u in range(first, last):
                cen = average(2, u)
                up = f[u] - cen
                lin[u] = lin[u] + gain[u] + up - cen
                gain[u] = up

    def pack_back(k, e, values):
        v = jnp.concatenate([round16(values(u)).astype(F32) for u in range(*RUNS[e])], axis=0)
        v = round16(sum(dot_0(order_e if e else order[...], term) for term in split(v)))
        snd = bufs[k][e][0]
        if e:
            for i in range(nc):
                snd[i] = fold(v[8 * i:8 * i + 8]).astype(I16)
        else:
            snd[...] = v.astype(I16).reshape(nc, ROWS, TILE)
        send_back(k, e)

    def give_back(e):
        pack_back(2, e, lambda u: (f[u] - 0.5) * FRAC_CODE)
        for u in range(*RUNS[e]):
            gain[u] += f[u] - average(4, u)
        pack_back(3, e, lambda u: gain[u] * GAIN_CODE)

    first_center(1)
    take_linear(1)
    step(1, 0)
    take_fraction(0)
    first_center(0)
    step(1, 1)
    take_linear(0)
    step(0, 0)
    step(1, 2)
    step(0, 1)
    step(1, 3)
    give_back(1)
    step(0, 2)
    step(0, 3)
    give_back(0)

    def home(k, e, write):
        wait_all(k, e, a_recv, bufs[k][e][1])
        rcv = bufs[k][e][1]
        n = nc * ROWS
        if e:
            v = jnp.concatenate([unfold(wide(rcv[j])) for j in range(nc)], axis=0)
            mat = back[:, n:]
        else:
            v = wide(rcv[...].reshape(n, TILE))
            mat = back[:, :n]
        m = sum(dot(mat, term) for term in split(v))
        for t in range(TL):
            write(slice(t * TILE, (t + 1) * TILE), m[t * HOME:(t + 1) * HOME])

    def write_f(ln, m):
        out_f[:, ln] = m * (1.0 / FRAC_CODE) + 0.5

    def write_d(ln, m):
        out_d[:, ln] = dual_v[:, ln] + m * (1.0 / GAIN_CODE)

    def add_f(ln, m):
        out_f[:, ln] += m * (1.0 / FRAC_CODE)

    def add_d(ln, m):
        out_d[:, ln] += m * (1.0 / GAIN_CODE)

    home(2, 1, write_f)
    home(3, 1, write_d)
    home(2, 0, add_f)
    home(3, 0, add_d)
    for k in range(4):
        for e in range(2):
            wait_all(k, e, a_send, bufs[k][e][0])
    for s in range(STEPS):
        for e in range(2):
            for side in range(2):
                part = halo.at[s, e, side]
                pltpu.make_async_copy(part, part, halo_send.at[s, e, side]).wait()


def body(start_fraction, ore_value, dual_price, patterns, cone_list, node_list, probability):
    ns, nc = lax.axis_size("space"), lax.axis_size("scen")
    blocks = start_fraction.shape[2]
    flat = (HOME, blocks)
    hbm = pl.BlockSpec(memory_space=pltpu.HBM)
    dma = pltpu.SemaphoreType.DMA
    v = pltpu.VMEM
    f, d = pl.pallas_call(
        functools.partial(kernel, ns, nc),
        out_shape=[v(flat, F32)] * 2,
        in_specs=[hbm] * 7,
        out_specs=[pl.BlockSpec(memory_space=v)] * 2,
        scratch_shapes=[
            pltpu.SMEM((2, TL, 3), jnp.int32),
            v((2, SCEN), jnp.int32),
            v((1, SCEN), F32),
            v(flat, BF16),
            v(flat, BF16),
            v(flat, F32),
            v((3, TILE, TILE), BF16),
            v((TL * HOME, TL * HOME), BF16),
            v((TL * HOME, TL * HOME), BF16),
            v((SCEN * MAIN, SCEN * MAIN), BF16),
            v((2, SCEN, SCEN), BF16),
            v((STEPS + 1, UNITS + 1, SCEN, TILE), BF16),
            v((STEPS, 2, 2, SCEN, TILE), BF16),
            v((UNITS, SCEN, TILE), F32),
            v((UNITS, SCEN, TILE), BF16),
            v((UNITS, SCEN, TILE), F32),
            v((UNITS, SCEN, TILE), F32),
            v((UNITS, SCEN, TILE), F32),
            *[v((nc, ROWS, TILE), kind) for kind in (BF16, BF16, *[I16] * 6)],
            *[v((nc, ROWS, HALF), kind) for kind in (BF16, BF16, *[I16] * 6)],
            v((2, TL, 3), jnp.int32),
            dma((7,)),
            dma((STEPS, 2, 2)),
            dma((STEPS, 2, 2)),
            dma((8,)),
            dma((8,)),
            dma((4,)),
        ],
        compiler_params=pltpu.CompilerParams(
            collective_id=0, has_side_effects=True, vmem_limit_bytes=56 * 2**20
        ),
    )(
        cone_list,
        node_list,
        probability.reshape(1, -1),
        start_fraction.reshape(flat),
        ore_value.reshape(flat),
        dual_price.reshape(flat),
        patterns,
    )
    return f.reshape(start_fraction.shape), d.reshape(start_fraction.shape)


def solution(mesh):
    in_specs = (
        P("scen", None, "space"),
        P("scen", None, "space"),
        P("scen", None, "space"),
        P(),
        P("space", None),
        P(),
        P(),
    )
    out_specs = (P("scen", None, "space"), P("scen", None, "space"))
    return jax.shard_map(body, mesh=mesh, in_specs=in_specs, out_specs=out_specs, check_vma=False)
```

time: 649 us -> 58.2 us (0.09)
  waiting for transfers between devices: 268 us -> 0 us
  blocking collectives: 160 us -> 0 us
  local copies, waits for them, and re-layouts: 108 us -> 1.76 us
  Pallas kernels: 0 us -> 55.7 us
  other arithmetic: 46.4 us -> 0 us
  matrix products: 25.3 us -> 0 us
  starting transfers between devices: 23.7 us -> 0 us
  between operations: 14.6 us -> 0.64 us
    psum x3 -> x0, waiting for transfers between devices: 258 us -> none  [tree_center(): lax.psum((root_term, first_term, second_term), 'scen')]
    psum x3 -> x0, blocking collectives: 160 us -> none  [tree_center(): lax.psum((root_term, first_term, second_term), 'scen')]
    pallas_call x0 -> x1, Pallas kernels: none -> 55.7 us  [body(): pl.pallas_call(functools.partial(kernel, ns, nc), out_shape=[v(flat, F32)...]
    gather x18 -> x0, local copies, waits for them, and re-layouts: 38.2 us -> none  [the longest x12 23.2 us: descend(): jnp.take(extended, local_cone[:, cone_slot], axis=2).reshape(-1, TILE)]
    reshape x20 -> x0, local copies, waits for them, and re-layouts: 28.6 us -> none  [the longest x12 13.9 us: descend(): jnp.take(extended, local_cone[:, cone_slot], axis=2).reshape(-1, TILE)]
    dot_general x21 -> x0, matrix products: 25.3 us -> none  [the longest x12 14.5 us: descend(): jnp.dot(picked, patterns[cone_slot], preferred_element_type=jnp.float32)]
    ppermute x8 -> x0, starting transfers between devices: 23.3 us -> none  [the longest x4 17.7 us: extended_2(): before = lax.ppermute(last, axis, up)]
    select_n x20 -> x0, other arithmetic: 16.2 us -> none  [the longest x14 8.87 us: descend(): jnp.take(extended, local_cone[:, cone_slot], axis=2).reshape(-1, TILE)]
  transfers between devices with their start and end apart: 11 -> 0, of which waited for: 7 -> 0; matrix products, arithmetic and copies ran while one was open for 9% -> 0% of each run, Pallas kernels for 0% -> 0%
where the time goes in v3:
time: 58.2 us; the launch traced here: 58.1 us
  Pallas kernels  55.7 us (96%)
  local copies, waits for them, and re-layouts  1.76 us (3%)
  between operations  0.64 us (1%)
    pallas_call x1, Pallas kernels, body(): pl.pallas_call(functools.partial(kernel, ns, nc), out_shape=[v(flat, F32)...  55.7 us
    unnamed x2, local copies, waits for them, and re-layouts  1.76 us

profile of v3, /device:TPU:1, one launch (start us, length us, event | category | flops | bytes accessed | tf_op | source)
XLA Modules:
  0.0 58.1 jit_solution(6389295095950414021)
XLA Ops:
  0.6 55.7 %shard_map.86 = (f32[96,2048]{1,0:T(8,128)S(1)}, f32[96,2048]{1,0:T(8,128)S(1)}) custom-call(s32[4,3]{1,0:T(4,128)} %cone_in.1, s32[2,64]{1,0:T(2,128)} %node_in.1, f32[1,64]{1,0:T(1,128)} %bitcast.11, bf16[96,2048]{1,0:T(8,128)(2,1)} %bitcast.9, bf16[96,2048]{1,0:T(8,128)(2,1)} %bitcast.10, f32[96,2048]{1,0:T(8,128)} %bitcast.8, bf16[3,512,512]{2,1,0:T(8,128)(2,1)} %pats_in.1), custom_call_target="tpu_custom_call" | custom-call | tf_op jit(solution)/shard_map/pallas_call | solution.py:430
  56.3 0.9 %copy.11 = f32[4,24,2048]{2,1,0:T(8,128)} copy(f32[4,24,2048]{2,1,0:T(8,128)S(1)} %bitcast.7) | data formatting | bytes 1572864
  57.2 0.9 %copy.12 = f32[4,24,2048]{2,1,0:T(8,128)} copy(f32[4,24,2048]{2,1,0:T(8,128)S(1)} %bitcast.6) | data formatting | bytes 1572864

commit v4 on v3

--- a/solution.py
+++ b/solution.py
@@ -133,15 +133,6 @@
         return jnp.where(jnp.where(which == 1, at_extra, at_main) == g, 1.0, 0.0).astype(BF16)
 
     perm[...] = places(1)
-    back[...] = places(0)
-
-    n = SCEN * MAIN
-    q, g = iota((n, 1), 0), iota((1, n), 1)
-    order_m = jnp.where(
-        ((q & (SCEN - 1)) >> 2) * ROWS + (q >> 6) * SCL + (q & 3) == g, 1.0, 0.0).astype(BF16)
-    q, g = iota((n // 2, 1), 0), iota((1, n // 2), 1)
-    order_e = jnp.where(
-        ((q & (SCEN - 1)) >> 2) * (ROWS // 2) + (q >> 6) * SCL + (q & 3) == g, 1.0, 0.0).astype(BF16)
 
     bufs = (
         ((snd_f, rcv_f), (snd_fe, rcv_fe)),
@@ -209,11 +200,22 @@
 
     load_f0.wait()
     pack(snd_f, snd_fe, [tiles(lambda ln: f0_v[:, ln])], lambda v: v)
+    pl.semaphore_wait(barrier, 2 * nc + 1)
+    send_out(0, 1)
+    send_out(0, 0)
+    load_cone.wait()
+    cone_copy = pltpu.make_async_remote_copy(
+        cone_v.at[0], cone_v.at[1], cone_sem.at[0], cone_sem.at[1],
+        device_id=(2 * z + 1 - yh, sc), device_id_type=MESH)
+    cone_copy.start()
+
     load_ore.wait()
     load_dual.wait()
 
     lin_home = tiles(lambda ln: jnp.round((dual_v[:, ln] - ore_v[:, ln].astype(F32)) * LIN_CODE))
     pack(snd_l, snd_le, split(lin_home), round16)
+    send_out(1, 1)
+    send_out(1, 0)
     load_node.wait()
     load_prob.wait()
     prob = prob_v[...]
@@ -229,17 +231,16 @@
         mean[k] = part
     for s in range(STEPS):
         rounded[s, UNITS] = jnp.zeros((SCEN, TILE), BF16)
+    n = SCEN * MAIN
+    q, g = iota((n, 1), 0), iota((1, n), 1)
+    order_m = jnp.where(
+        ((q & (SCEN - 1)) >> 2) * ROWS + (q >> 6) * SCL + (q & 3) == g, 1.0, 0.0).astype(BF16)
+    q, g = iota((n // 2, 1), 0), iota((1, n // 2), 1)
+    order_e = jnp.where(
+        ((q & (SCEN - 1)) >> 2) * (ROWS // 2) + (q >> 6) * SCL + (q & 3) == g, 1.0, 0.0).astype(BF16)
+
     order[...] = order_m
-
-    pl.semaphore_wait(barrier, 2 * nc + 1)
-    for e in (1, 0):
-        for k in range(2):
-            send_out(k, e)
-    load_cone.wait()
-    cone_copy = pltpu.make_async_remote_copy(
-        cone_v.at[0], cone_v.at[1], cone_sem.at[0], cone_sem.at[1],
-        device_id=(2 * z + 1 - yh, sc), device_id_type=MESH)
-    cone_copy.start()
+    back[...] = places(0)
 
     def start_halo(step, e, u, side, to):
         pltpu.make_async_remote_copy(
@@ -418,6 +419,18 @@
             for side in range(2):
                 part = halo.at[s, e, side]
                 pltpu.make_async_copy(part, part, halo_send.at[s, e, side]).wait()
+
+
+def store(f, d, f_out, d_out, sem):
+    copies = []
+    for k in range(4):
+        rows = pl.ds(k * PER, PER)
+        copies.append(pltpu.make_async_copy(f.at[rows], f_out.at[rows], sem.at[2 * k]))
+        copies.append(pltpu.make_async_copy(d.at[rows], d_out.at[rows], sem.at[2 * k + 1]))
+    for c in copies:
+        c.start()
+    for c in copies:
+        c.wait()
 
 
 def body(start_fraction, ore_value, dual_price, patterns, cone_list, node_list, probability):
@@ -473,6 +486,14 @@
         dual_price.reshape(flat),
         patterns,
     )
+    f, d = pl.pallas_call(
+        store,
+        out_shape=[jax.ShapeDtypeStruct(flat, F32)] * 2,
+        in_specs=[pl.BlockSpec(memory_space=pl.ANY)] * 2,
+        out_specs=[hbm] * 2,
+        scratch_shapes=[dma((8,))],
+        compiler_params=pltpu.CompilerParams(vmem_limit_bytes=4 * 2**20),
+    )(f, d)
     return f.reshape(start_fraction.shape), d.reshape(start_fraction.shape)
 
 

time: 58.2 us -> 57.6 us (0.990)
  local copies, waits for them, and re-layouts: 1.76 us -> 0 us
  Pallas kernels: 55.7 us -> 56.9 us
    unnamed x2 -> x0, local copies, waits for them, and re-layouts: 1.76 us -> none
    pallas_call x0 -> x1, Pallas kernels: none -> 1.2 us  [body(): pl.pallas_call(store, out_shape=[jax.ShapeDtypeStruct(flat, F32)] * 2, in...]
where the time goes in v4:
time: 57.6 us; the launch traced here: 57.5 us
  Pallas kernels  56.9 us (99%)
  between operations  0.64 us (1%)
    pallas_call x1, Pallas kernels, body(): pl.pallas_call(functools.partial(kernel, ns, nc), out_shape=[v(flat, F32)...  55.7 us
    pallas_call x1, Pallas kernels, body(): pl.pallas_call(store, out_shape=[jax.ShapeDtypeStruct(flat, F32)] * 2, in...  1.2 us

profile of v4, /device:TPU:1, one launch (start us, length us, event | category | flops | bytes accessed | tf_op | source)
XLA Modules:
  0.0 57.5 jit_solution(10872229233118400109)
XLA Ops:
  0.6 55.7 %shard_map.86 = (f32[96,2048]{1,0:T(8,128)S(1)}, f32[96,2048]{1,0:T(8,128)S(1)}) custom-call(s32[4,3]{1,0:T(4,128)} %cone_in.1, s32[2,64]{1,0:T(2,128)} %node_in.1, f32[1,64]{1,0:T(1,128)} %bitcast.9, bf16[96,2048]{1,0:T(8,128)(2,1)} %bitcast.7, bf16[96,2048]{1,0:T(8,128)(2,1)} %bitcast.8, f32[96,2048]{1,0:T(8,128)} %bitcast.6, bf16[3,512,512]{2,1,0:T(8,128)(2,1)} %pats_in.1), custom_call_target="tpu_custom_call" | custom-call | tf_op jit(solution)/shard_map/pallas_call | solution.py:443
  56.3 1.2 %shard_map.87 = (f32[96,2048]{1,0:T(8,128)}, f32[96,2048]{1,0:T(8,128)}) custom-call(f32[96,2048]{1,0:T(8,128)S(1)} %get-tuple-element.6.f, f32[96,2048]{1,0:T(8,128)S(1)} %get-tuple-element.7.d), custom_call_target="tpu_custom_call" | custom-call | tf_op jit(solution)/shard_map/pallas_call | solution.py:489
